TPU v7x, 512 devices: a whole 4x4x16 slice. The times are simulated.
512 devices in a mesh: pipe: 4 (over z_hi), dp: 16 (over y, x), tensor: 8 (over z_lo, core).
Axes of the slice: x: 4, y: 4, z: 16 (z_hi: 4, z_lo: 4; z = z_hi * 4 + z_lo), core: 2. Of those that a mesh axis runs over, the one named last changes fastest.
Arguments:
- x_in: bfloat16 [4, 2, 16, 128, 1600], P('pipe', None, 'dp', 'tensor'), may hold values from -6 to 6
- out_grad: bfloat16 [2, 16, 128, 1600], P(None, 'dp'), may hold values from -6 to 6
- layer_scale: float32 [4, 1600], P('pipe'), may hold values from 0.05 to 1
- norm_gain: float32 [4, 1600], P('pipe'), may hold values from 0.5 to 1.5
- master: float32 [4, 1600, 8192], P('pipe', 'dp', 'tensor'), may hold values from -0.15625 to 0.15625
- moment_one: float32 [4, 1600, 8192], P('pipe', 'dp', 'tensor'), may hold values from -4 to 4
- moment_two: float32 [4, 1600, 8192], P('pipe', 'dp', 'tensor'), may hold values from 0.05 to 5
Outputs:
- input_grads: bfloat16 [4, 2, 16, 128, 1600], P('pipe', None, 'dp', 'tensor')
- new_master: float32 [4, 1600, 8192], P('pipe', 'dp', 'tensor')
- new_moment_one: float32 [4, 1600, 8192], P('pipe', 'dp', 'tensor')
- new_moment_two: float32 [4, 1600, 8192], P('pipe', 'dp', 'tensor')
- scale_grads: float32 [4, 2, 1600], P('pipe')
All inputs are finite; a program needn't handle non-finite values.
Results may differ from a plain program's by a relative error of at most 0.027.
Values may be sent and summed in bfloat16 or wider, within the bound.
A program may use at most 128 MiB of HBM per device.

v0:
```python
import math
import jax
import jax.numpy as jnp
from jax import lax
from jax.sharding import PartitionSpec as P

HD = 128
beta_one = 0.9
beta_two = 0.95
adam_eps = 1e-08
learn_rate = 0.001
weight_decay = 0.05
adam_step = 100.0
norm_eps = 1e-06


def from_behind(block, axis, distance):
    devices = range(lax.axis_size(axis))
    route = [(i - distance, i) for i in devices if i - distance in devices]
    return lax.ppermute(block, axis, route)


def normalize(values_in):
    inverse = lax.rsqrt(jnp.mean(values_in * values_in, axis=-1, keepdims=True) + norm_eps)
    return (inverse, values_in * inverse)


def select_micro(array, micro_index):
    return lax.dynamic_index_in_dim(array, micro_index, 0, keepdims=False)


def store_slot(buffer, value, slot_index):
    return lax.dynamic_update_index_in_dim(buffer, value, slot_index, 0)


def local(x_in, out_grad, layer_scale, norm_gain, master, moment_one, moment_two):
    n_pipe = lax.axis_size("pipe")
    n_tensor = lax.axis_size("tensor")
    pipe_rank = lax.axis_index("pipe")
    micro_count = x_in.shape[1]
    images = x_in.shape[2]
    shard_len = x_in.shape[3]
    channels = x_in.shape[4]
    seq_len = shard_len * n_tensor
    row_start = lax.axis_index("tensor") * shard_len
    head_cols = master.shape[2] // 4
    local_heads = head_cols // HD
    score_root = math.sqrt(HD)
    scale_vec = layer_scale[0]
    gain_vec = norm_gain[0]
    weights = lax.all_gather(master[0].astype(jnp.bfloat16), "dp", axis=0, tiled=True)
    w_qkv = weights[:, : 3 * head_cols]
    w_out = weights[:, 3 * head_cols :]
    full_x = lax.all_gather(x_in[0], "tensor", axis=2, tiled=True).astype(jnp.float32)
    full_inverse, full_unit = normalize(full_x)
    normed = (full_unit * gain_vec).astype(jnp.bfloat16)
    local_unit = lax.dynamic_slice_in_dim(full_unit, row_start, shard_len, 2)
    local_inverse = lax.dynamic_slice_in_dim(full_inverse, row_start, shard_len, 2)
    projected = jnp.einsum(
        "mbsd,dc->mbsc", normed, w_qkv, preferred_element_type=jnp.float32
    ).astype(jnp.bfloat16)
    projected = projected.reshape(micro_count, images, seq_len, 3, local_heads, HD)
    query = projected[:, :, :, 0]
    keys = projected[:, :, :, 1]
    values = projected[:, :, :, 2]
    scores = (
        jnp.einsum("mbqhe,mbkhe->mbhqk", query, keys, preferred_element_type=jnp.float32)
        / score_root
    )
    probs = jax.nn.softmax(scores, axis=-1)
    probs_low = probs.astype(jnp.bfloat16)
    attended = jnp.einsum(
        "mbhqk,mbkhe->mbqhe", probs_low, values, preferred_element_type=jnp.float32
    ).astype(jnp.bfloat16)
    attended_flat = attended.reshape(micro_count, images, seq_len, head_cols)

    def backward_segment(micro_index, incoming):
        query_now = select_micro(query, micro_index)
        keys_now = select_micro(keys, micro_index)
        values_now = select_micro(values, micro_index)
        probs_now = select_micro(probs, micro_index)
        probs_low_now = select_micro(probs_low, micro_index)
        attended_now = select_micro(attended, micro_index)
        scaled = (scale_vec * incoming.astype(jnp.float32)).astype(jnp.bfloat16)
        d_att = jnp.einsum("bsd,dc->bsc", scaled, w_out, preferred_element_type=jnp.float32).astype(
            jnp.bfloat16
        )
        d_att = d_att.reshape(images, seq_len, local_heads, HD)
        d_prob = jnp.einsum(
            "bqhe,bkhe->bhqk", d_att, values_now, preferred_element_type=jnp.float32
        )
        row_delta = jnp.einsum(
            "bqhe,bqhe->bhq", d_att, attended_now, preferred_element_type=jnp.float32
        )
        d_score = (probs_now * (d_prob - row_delta[..., None]) / score_root).astype(jnp.bfloat16)
        d_query = jnp.einsum(
            "bhqk,bkhe->bqhe", d_score, keys_now, preferred_element_type=jnp.float32
        ).astype(jnp.bfloat16)
        d_keys = jnp.einsum(
            "bhqk,bqhe->bkhe", d_score, query_now, preferred_element_type=jnp.float32
        ).astype(jnp.bfloat16)
        d_values = jnp.einsum(
            "bhqk,bqhe->bkhe", probs_low_now, d_att, preferred_element_type=jnp.float32
        ).astype(jnp.bfloat16)
        d_proj = jnp.concatenate([d_query, d_keys, d_values], axis=2).reshape(
            images, seq_len, 3 * head_cols
        )
        partial_sum = jnp.einsum("bsc,dc->bsd", d_proj, w_qkv, preferred_element_type=jnp.float32)
        return (partial_sum, d_proj, scaled)

    def spare_segment(micro_index, incoming):
        return (
            jnp.zeros((images, seq_len, channels), jnp.float32),
            jnp.zeros((images, seq_len, 3 * head_cols), jnp.bfloat16),
            jnp.zeros((images, seq_len, channels), jnp.bfloat16),
        )

    segments = n_pipe + micro_count - 1
    is_last = pipe_rank == n_pipe - 1
    received = jnp.zeros((images, seq_len, channels), jnp.bfloat16)
    slots = micro_count + 1
    grads_out = jnp.zeros((slots, images, shard_len, channels), jnp.bfloat16)
    proj_saved = jnp.zeros((slots, images, seq_len, 3 * head_cols), jnp.bfloat16)
    scaled_saved = jnp.zeros((slots, images, seq_len, channels), jnp.bfloat16)
    grad_saved = jnp.zeros((slots, images, seq_len, channels), jnp.bfloat16)
    gain_part = jnp.zeros((channels,), jnp.float32)
    for segment_step in range(segments):
        micro_index = segment_step - (n_pipe - 1) + pipe_rank
        active = jnp.logical_and(micro_index >= 0, micro_index < micro_count)
        micro_index = jnp.clip(micro_index, 0, micro_count - 1)
        slot_index = jnp.where(active, micro_index, micro_count)
        arrived = received
        incoming = jnp.where(is_last, select_micro(out_grad, micro_index), arrived)
        partial_sum, d_proj, scaled = lax.cond(
            active, backward_segment, spare_segment, micro_index, incoming
        )
        pieces = partial_sum.astype(jnp.bfloat16).reshape(images, n_tensor, shard_len, channels)
        landed = lax.all_to_all(pieces, "tensor", split_axis=1, concat_axis=1, tiled=True)
        own_d = jnp.sum(landed.astype(jnp.float32), axis=1)
        own_unit = select_micro(local_unit, micro_index)
        own_inverse = select_micro(local_inverse, micro_index)
        d_unit = own_d * gain_vec
        d_input = own_inverse * (
            d_unit - own_unit * jnp.mean(d_unit * own_unit, axis=-1, keepdims=True)
        )
        own_incoming = lax.dynamic_slice_in_dim(incoming, row_start, shard_len, 1)
        own_passed = (own_incoming.astype(jnp.float32) + d_input).astype(jnp.bfloat16)
        gain_part = gain_part + jnp.where(active, jnp.sum(own_d * own_unit, axis=(0, 1)), 0.0)
        grads_out = store_slot(grads_out, own_passed, slot_index)
        proj_saved = store_slot(proj_saved, d_proj, slot_index)
        scaled_saved = store_slot(scaled_saved, scaled, slot_index)
        grad_saved = store_slot(grad_saved, incoming, slot_index)
        if segment_step + 1 < segments:
            moved = from_behind(own_passed, "pipe", -1)
            received = lax.all_gather(moved, "tensor", axis=1, tiled=True)
    grads_kept = grads_out[:micro_count]
    proj_kept = proj_saved[:micro_count]
    scaled_kept = scaled_saved[:micro_count]
    grad_kept = grad_saved[:micro_count]
    grad_qkv = jnp.einsum("mbsd,mbsc->dc", normed, proj_kept, preferred_element_type=jnp.float32)
    grad_out = jnp.einsum(
        "mbsd,mbsc->dc", scaled_kept, attended_flat, preferred_element_type=jnp.float32
    )
    weight_grad = lax.psum_scatter(
        jnp.concatenate([grad_qkv, grad_out], axis=1).astype(jnp.bfloat16),
        "dp",
        scatter_dimension=0,
        tiled=True,
    ).astype(jnp.float32)
    summed_out = jnp.einsum(
        "mbsd,mbsc->dc", grad_kept, attended_flat, preferred_element_type=jnp.float32
    )
    scale_part = jnp.sum(w_out.astype(jnp.float32) * summed_out, axis=1)
    scale_both = lax.psum(lax.psum(jnp.stack([scale_part, gain_part]), "tensor"), "dp")
    bias_one = 1.0 - beta_one**adam_step
    bias_two = 1.0 - beta_two**adam_step
    first_new = beta_one * moment_one[0] + (1.0 - beta_one) * weight_grad
    second_new = beta_two * moment_two[0] + (1.0 - beta_two) * weight_grad * weight_grad
    update = first_new / bias_one / (jnp.sqrt(second_new / bias_two) + adam_eps)
    master_new = master[0] - learn_rate * (update + weight_decay * master[0])
    return (grads_kept[None], master_new[None], first_new[None], second_new[None], scale_both[None])


def solution(mesh):
    placed = (
        P("pipe", None, "dp", "tensor", None),
        P(None, "dp", None, None),
        P("pipe", None),
        P("pipe", None),
        P("pipe", "dp", "tensor"),
        P("pipe", "dp", "tensor"),
        P("pipe", "dp", "tensor"),
    )
    return jax.shard_map(
        local,
        mesh=mesh,
        in_specs=placed,
        out_specs=(
            P("pipe", None, "dp", "tensor", None),
            P("pipe", "dp", "tensor"),
            P("pipe", "dp", "tensor"),
            P("pipe", "dp", "tensor"),
            P("pipe", None, None),
        ),
        check_vma=False,
    )
```

profile of v0, /device:TPU:128, one launch (start us, length us, event | category | flops | bytes accessed | tf_op | source)
XLA Modules:
  0.0 831.2 jit_solution(14182584001447104835)
XLA Ops:
  9.8 17.2 %all-gather = bf16[1,2,1,128,1600]{4,3,2,1,0:T(8,128)(2,1)S(1)} all-gather(bf16[1,2,1,16,1600]{4,3,2,1,0:T(8,128)(2,1)} %param.17), channel_id=2, replica_groups=mesh['pipe'=4,'dp'=16,'tensor'=8] {'tensor'}, dimensions={3}, use_global_device_ids=true | all-gather | bytes 921600 | tf_op jit(solution)/shard_map/all_gather | solution.py:54
  28.4 50.3 %all-gather.4.cloned.1.call-done = bf16[16,100,1024]{2,1,0:T(8,128)(2,1)} async-done(((bf16[1,100,1024]{2,1,0:T(8,128)(2,1)}), bf16[16,100,1024]{2,1,0:T(8,128)(2,1)}) %all-gather.4.cloned.1.call-update) | async-done | bytes 3276816 | tf_op jit(solution)/shard_map/all_gather | solution.py:51
  78.8 4.5 reshape.1362
  84.5 2.6 fusion.115
  95.5 2.3 conditional.5
  99.8 4.8 all-to-all-start
  106.1 2.5 convert_multiply_fusion.6
  108.6 9.3 %all-to-all-done = bf16[1,8,16,1600]{3,2,0,1:T(8,128)(2,1)} async-done(((bf16[1,8,16,1600]{3,2,0,1:T(8,128)(2,1)}), bf16[1,8,16,1600]{3,2,0,1:T(8,128)(2,1)}, u32[]{:S(2)}, u32[]{:S(2)}) %all-to-all-start) | async-done | bytes 409632 | tf_op jit(solution)/shard_map/all_to_all | solution.py:138
  121.8 2.2 fusion.165
  128.0 2.2 fusion.121
  130.1 2.1 collective-permute-start
  132.2 40.1 %collective-permute-done = bf16[1,16,1600]{1,2,0:T(8,128)(2,1)} collective-permute-done((bf16[1,16,1600]{1,2,0:T(8,128)(2,1)}, bf16[1,16,1600]{1,2,0:T(8,128)(2,1)}, u32[]{:S(2)}, u32[]{:S(2)}) %collective-permute-start) | collective-permute-done | bytes 51232 | tf_op jit(solution)/shard_map/ppermute | solution.py:20
  174.1 15.8 %all_gather.20 = bf16[1,128,1600]{2,1,0:T(8,128)(2,1)} all-gather(bf16[1,16,1600]{2,1,0:T(8,128)(2,1)} %copy.219), channel_id=1, replica_groups=mesh['pipe'=4,'dp'=16,'tensor'=8] {'tensor'}, dimensions={1}, use_global_device_ids=true | all-gather | bytes 460800 | tf_op jit(solution)/shard_map/all_gather | solution.py:155
  191.9 2.1 bitcast_dynamic-update-slice_fusion.2
  194.0 2.7 conditional.6
  198.7 16.6 %all_to_all.25 = bf16[1,8,16,1600]{3,2,0,1:T(8,128)(2,1)S(1)} all-to-all(bf16[1,8,16,1600]{3,2,0,1:T(8,128)(2,1)} %bitcast.592), channel_id=1, replica_groups=mesh['pipe'=4,'dp'=16,'tensor'=8] {'tensor'}, dimensions={1} | all-to-all | bytes 819200 | tf_op jit(solution)/shard_map/all_to_all | solution.py:138
  216.1 2.2 fusion.164
  224.3 2.2 fusion.141
  226.4 2.2 collective-permute-start.1
  228.6 94.0 %collective-permute-done.1 = bf16[1,16,1600]{1,2,0:T(8,128)(2,1)} collective-permute-done((bf16[1,16,1600]{1,2,0:T(8,128)(2,1)}, bf16[1,16,1600]{1,2,0:T(8,128)(2,1)}, u32[]{:S(2)}, u32[]{:S(2)}) %collective-permute-start.1) | collective-permute-done | bytes 51232 | tf_op jit(solution)/shard_map/ppermute | solution.py:20
  324.4 15.8 %all_gather.21 = bf16[1,128,1600]{2,1,0:T(8,128)(2,1)} all-gather(bf16[1,16,1600]{2,1,0:T(8,128)(2,1)} %copy.234), channel_id=1, replica_groups=mesh['pipe'=4,'dp'=16,'tensor'=8] {'tensor'}, dimensions={1}, use_global_device_ids=true | all-gather | bytes 460800 | tf_op jit(solution)/shard_map/all_gather | solution.py:155
  342.2 2.1 bitcast_dynamic-update-slice_fusion.1
  344.3 32.0 %conditional.7 = (bf16[1,128,1600]{1,2,0:T(8,128)(2,1)}, bf16[1,1,128,768]{3,2,0,1:T(8,128)(2,1)}, bf16[1,1,128,1600]{2,3,0,1:T(8,128)(2,1)}) conditional(s32[]{:T(128)} %convert_element_type.339, () %tuple.72, (s32[]{:T(128)}, bf16[2,1,128,2,128]{4,2,3,0,1:T(8,128)(2,1)}, f32[2,1,2,128,128]{3,4,2,0,1:T(8,128)S(1)}, f32[1,1600]{1,0:T(1,128)S(1)}, ...), branch_computations={%region_11.12_spmd, %region_12.13_spmd} | conditional | flops 454803200 | bytes 11565162 | solution.py:134
  378.3 4.1 all-to-all-start.2
  391.7 4.0 all-to-all-done.2
  397.4 2.2 fusion.163
  399.6 2.1 copy.246
  401.7 2.2 copy.247
  411.1 38.8 %collective-permute-done.2 = bf16[1,16,1600]{1,2,0:T(8,128)(2,1)} collective-permute-done((bf16[1,16,1600]{1,2,0:T(8,128)(2,1)S(1)}, bf16[1,16,1600]{1,2,0:T(8,128)(2,1)}, u32[]{:S(2)}, u32[]{:S(2)}) %collective-permute-start.2) | collective-permute-done | bytes 51232 | tf_op jit(solution)/shard_map/ppermute | solution.py:20
  451.8 15.8 %all_gather.22 = bf16[1,128,1600]{2,1,0:T(8,128)(2,1)} all-gather(bf16[1,16,1600]{2,1,0:T(8,128)(2,1)} %copy.249), channel_id=1, replica_groups=mesh['pipe'=4,'dp'=16,'tensor'=8] {'tensor'}, dimensions={1}, use_global_device_ids=true | all-gather | bytes 460800 | tf_op jit(solution)/shard_map/all_gather | solution.py:155
  469.5 2.1 bitcast_dynamic-update-slice_fusion
  471.6 32.2 %conditional.8 = (bf16[1,128,1600]{1,2,0:T(8,128)(2,1)}, bf16[1,1,128,768]{3,2,0,1:T(8,128)(2,1)}, bf16[1,1,128,1600]{2,3,0,1:T(8,128)(2,1)}) conditional(s32[]{:T(128)} %convert_element_type.344, () %tuple.74, (s32[]{:T(128)}, bf16[2,1,128,2,128]{4,2,3,0,1:T(8,128)(2,1)}, f32[2,1,2,128,128]{3,4,2,0,1:T(8,128)S(1)}, f32[1,1600]{1,0:T(1,128)S(1)}, ...), branch_computations={%region_15.16_spmd, %region_16.17_spmd} | conditional | flops 454803200 | bytes 11565162 | solution.py:134
  505.9 4.1 all-to-all-start.3
  528.4 2.2 fusion.162
  530.6 2.1 copy.261
  532.7 2.2 copy.262
  536.7 2.2 fusion.131
  538.9 2.2 collective-permute-start.3
  544.3 14.5 %collective-permute-done.3 = bf16[1,16,1600]{1,2,0:T(8,128)(2,1)} collective-permute-done((bf16[1,16,1600]{1,2,0:T(8,128)(2,1)}, bf16[1,16,1600]{1,2,0:T(8,128)(2,1)}, u32[]{:S(2)}, u32[]{:S(2)}) %collective-permute-start.3) | collective-permute-done | bytes 51232 | tf_op jit(solution)/shard_map/ppermute | solution.py:20
  560.6 37.5 %all_gather.23 = bf16[1,128,1600]{2,1,0:T(8,128)(2,1)} all-gather(bf16[1,16,1600]{2,1,0:T(8,128)(2,1)} %copy.264), channel_id=1, replica_groups=mesh['pipe'=4,'dp'=16,'tensor'=8] {'tensor'}, dimensions={1}, use_global_device_ids=true | all-gather | bytes 460800 | tf_op jit(solution)/shard_map/all_gather | solution.py:155
  600.0 2.1 bitcast_dynamic-update-slice_fusion.3
  602.1 2.3 conditional.9
  606.5 5.1 all-to-all-start.4
  619.0 85.0 %fusion = bf16[112,1024]{1,0:T(8,128)(2,1)} fusion(bf16[1600,1024]{1,0:T(8,128)(2,1)S(1)} %pad_maximum_fusion.5), kind=kCustom, calls=%all-reduce-scatter | all-reduce-scatter fusion | flops 1835009 | bytes 3508224
  705.0 3.7 collective-permute-start.4
  708.6 4.1 collective-permute-start.5
  722.6 27.0 %psum.14 = f32[2,1600]{1,0:T(2,128)S(1)} all-reduce(f32[2,1600]{1,0:T(2,128)S(1)} %pad_maximum_fusion.6), channel_id=1, replica_groups=mesh['pipe'=4,'dp'=16,'tensor'=8] {'tensor'}, use_global_device_ids=true, to_apply=%region_30.31 | all-reduce | flops 3200 | bytes 25600 | tf_op jit(solution)/shard_map/psum | solution.py:174
  749.6 71.2 %psum.15 = f32[1,2,1600]{2,1,0:T(2,128)} all-reduce(f32[1,2,1600]{2,1,0:T(2,128)S(1)} %bitcast.594), channel_id=1, replica_groups=mesh['pipe'=4,'dp'=16,'tensor'=8] {'dp'}, use_global_device_ids=true, to_apply=%region_31.32 | all-reduce | flops 3200 | bytes 25600 | tf_op jit(solution)/shard_map/psum | solution.py:174
  (224 shorter events, 187.9 us)
Async XLA Ops:
  7.2 71.6 %all-gather.4.cloned.1.call-start = ((), (), s32[]{:S(2)}) async-start(), calls=%async_computation.5 | async-start | bytes 3620864 | tf_op jit(solution)/shard_map/all_gather | solution.py:51
  9.0 18.5 %copy-start.10 = (bf16[2,1,128,1600]{2,3,1,0:T(8,128)(2,1)S(1)}, bf16[2,1,128,1600]{2,3,1,0:T(8,128)(2,1)}, u32[]{:S(2)}) copy-start(bf16[2,1,128,1600]{2,3,1,0:T(8,128)(2,1)} %param.18) | copy-start | bytes 2457604
  27.0 57.4 %copy-start = (bf16[1,2,1,128,1600]{4,3,2,1,0:T(8,128)(2,1)}, bf16[1,2,1,128,1600]{4,3,2,1,0:T(8,128)(2,1)S(1)}, u32[]{:S(2)}) copy-start(bf16[1,2,1,128,1600]{4,3,2,1,0:T(8,128)(2,1)S(1)} %all-gather) | copy-start | bytes 2457604
  27.3 57.2 %copy-start.39 = (f32[2,128]{1,0:T(2,128)}, f32[2,128]{1,0:T(2,128)S(1)}, u32[]{:S(2)}) copy-start(f32[2,128]{1,0:T(2,128)S(1)} %add_rsqrt_fusion) | copy-start | bytes 3076
  28.4 50.4 %copy-start.21 = (bf16[3,1,128,1600]{2,3,0,1:T(8,128)(2,1)}, bf16[3,1,128,1600]{2,3,0,1:T(8,128)(2,1)S(1)}, u32[]{:S(2)}) copy-start(bf16[3,1,128,1600]{2,3,0,1:T(8,128)(2,1)S(1)} %get-tuple-element.409) | copy-start | bytes 3686404
  87.5 0.8 copy-start.27
  87.5 4.2 copy-start.26
  91.7 3.9 copy-start.33
  91.8 2.1 copy-start.12
  99.8 18.2 %all-to-all-start = ((bf16[1,8,16,1600]{3,2,0,1:T(8,128)(2,1)}), bf16[1,8,16,1600]{3,2,0,1:T(8,128)(2,1)}, u32[]{:S(2)}, u32[]{:S(2)}) async-start(bf16[1,8,16,1600]{3,2,0,1:T(8,128)(2,1)} %bitcast.589), calls=%async_computation | async-start | bytes 851968 | tf_op jit(solution)/shard_map/all_to_all | solution.py:138
  126.1 1.8 copy-start.2
  126.1 1.9 copy-start.6
  130.1 42.2 %collective-permute-start = (bf16[1,16,1600]{1,2,0:T(8,128)(2,1)}, bf16[1,16,1600]{1,2,0:T(8,128)(2,1)}, u32[]{:S(2)}, u32[]{:S(2)}) collective-permute-start(bf16[1,16,1600]{1,2,0:T(8,128)(2,1)} %fusion.121), channel_id=1, source_target_pairs={{128,0},{256,128},{384,256},{129,1},{257,129},{385,257},{130,2},{2... | collective-permute-start | bytes 153608 | tf_op jit(solution)/shard_map/ppermute | solution.py:20
  215.4 0.7 copy-start.22
  222.4 1.8 copy-start.3
  222.4 1.9 copy-start.7
  226.4 96.2 %collective-permute-start.1 = (bf16[1,16,1600]{1,2,0:T(8,128)(2,1)}, bf16[1,16,1600]{1,2,0:T(8,128)(2,1)}, u32[]{:S(2)}, u32[]{:S(2)}) collective-permute-start(bf16[1,16,1600]{1,2,0:T(8,128)(2,1)} %fusion.141), channel_id=1, source_target_pairs={{128,0},{256,128},{384,256},{129,1},{257,129},{385,257},{130,2},{2... | collective-permute-start | bytes 153608 | tf_op jit(solution)/shard_map/ppermute | solution.py:20
  372.3 0.7 copy-start.16
  378.3 17.4 %all-to-all-start.2 = ((bf16[1,8,16,1600]{3,2,0,1:T(8,128)(2,1)}), bf16[1,8,16,1600]{3,2,0,1:T(8,128)(2,1)}, u32[]{:S(2)}, u32[]{:S(2)}) async-start(bf16[1,8,16,1600]{3,2,0,1:T(8,128)(2,1)} %bitcast.590), calls=%async_computation.2 | async-start | bytes 851968 | tf_op jit(solution)/shard_map/all_to_all | solution.py:138
  396.8 0.6 copy-start.23
  403.9 1.8 copy-start.4
  403.9 1.9 copy-start.8
  405.7 4.8 copy-start.32
  407.2 0.8 copy-start.18
  407.9 42.0 %collective-permute-start.2 = (bf16[1,16,1600]{1,2,0:T(8,128)(2,1)S(1)}, bf16[1,16,1600]{1,2,0:T(8,128)(2,1)}, u32[]{:S(2)}, u32[]{:S(2)}) collective-permute-start(bf16[1,16,1600]{1,2,0:T(8,128)(2,1)S(1)} %fusion.136), channel_id=1, source_target_pairs={{128,0},{256,128},{384,256},{129,1},{257,129},{385,257},{130,2},{2... | collective-permute-start | bytes 153608 | tf_op jit(solution)/shard_map/ppermute | solution.py:20
  499.9 0.7 copy-start.17
  505.9 20.8 %all-to-all-start.3 = ((bf16[1,8,16,1600]{3,2,0,1:T(8,128)(2,1)}), bf16[1,8,16,1600]{3,2,0,1:T(8,128)(2,1)}, u32[]{:S(2)}, u32[]{:S(2)}) async-start(bf16[1,8,16,1600]{3,2,0,1:T(8,128)(2,1)} %bitcast.591), calls=%async_computation.3 | async-start | bytes 851968 | tf_op jit(solution)/shard_map/all_to_all | solution.py:138
  527.8 0.6 copy-start.24
  534.8 1.8 copy-start.5
  534.8 1.9 copy-start.9
  538.9 19.9 %collective-permute-start.3 = (bf16[1,16,1600]{1,2,0:T(8,128)(2,1)}, bf16[1,16,1600]{1,2,0:T(8,128)(2,1)}, u32[]{:S(2)}, u32[]{:S(2)}) collective-permute-start(bf16[1,16,1600]{1,2,0:T(8,128)(2,1)} %fusion.131), channel_id=1, source_target_pairs={{128,0},{256,128},{384,256},{129,1},{257,129},{385,257},{130,2},{2... | collective-permute-start | bytes 153608 | tf_op jit(solution)/shard_map/ppermute | solution.py:20
  604.4 8.8 %copy-start.1 = (bf16[1,2,1,128,1600]{4,3,2,1,0:T(8,128)(2,1)S(1)}, bf16[1,2,1,128,1600]{4,3,2,1,0:T(8,128)(2,1)}, u32[]{:S(2)}) copy-start(bf16[1,2,1,128,1600]{4,3,2,1,0:T(8,128)(2,1)} %copy-done) | copy-start | bytes 2457604
  604.4 8.8 %copy-start.40 = (f32[2,128]{1,0:T(2,128)S(1)}, f32[2,128]{1,0:T(2,128)}, u32[]{:S(2)}) copy-start(f32[2,128]{1,0:T(2,128)} %copy-done.39) | copy-start | bytes 3076
  606.5 113.7 %all-to-all-start.4 = ((bf16[1,8,16,1600]{3,2,0,1:T(8,128)(2,1)}), bf16[1,8,16,1600]{3,2,0,1:T(8,128)(2,1)}, u32[]{:S(2)}, u32[]{:S(2)}) async-start(bf16[1,8,16,1600]{3,2,0,1:T(8,128)(2,1)} %bitcast.152), calls=%async_computation.4 | async-start | bytes 851968 | tf_op jit(solution)/shard_map/all_to_all | solution.py:138
  613.2 3.7 copy-start.11
  704.0 11.5 %copy-start.20 = (bf16[112,1024]{1,0:T(8,128)(2,1)S(1)}, bf16[112,1024]{1,0:T(8,128)(2,1)}, u32[]{:S(2)}) copy-start(bf16[112,1024]{1,0:T(8,128)(2,1)} %fusion) | copy-start | bytes 688132
  705.0 10.5 %collective-permute-start.4 = (bf16[112,1024]{1,0:T(8,128)(2,1)}, bf16[112,1024]{1,0:T(8,128)(2,1)S(1)}, u32[]{:S(2)}, u32[]{:S(2)}) collective-permute-start(bf16[112,1024]{1,0:T(8,128)(2,1)} %fusion), channel_id=1, source_target_pairs={{0,8},{8,16},{16,24},{24,32},{32,40},{40,48},{48,56},{56,64},{64,7... | collective-permute-start | bytes 688136
  708.6 6.8 collective-permute-start.5
  712.7 3.4 copy-start.19
  712.7 3.4 copy-start.28
  712.7 3.4 copy-start.29
  717.8 4.7 copy-start.35
  717.8 4.7 copy-start.36
  717.8 4.7 copy-start.37
  717.8 4.7 copy-start.38
  722.2 99.2 %copy-start.13 = (bf16[1,128,1600]{1,2,0:T(8,128)(2,1)S(1)}, bf16[1,128,1600]{1,2,0:T(8,128)(2,1)}, u32[]{:S(2)}) copy-start(bf16[1,128,1600]{1,2,0:T(8,128)(2,1)} %get-tuple-element.402) | copy-start | bytes 1228804
  722.2 99.2 %copy-start.41 = (f32[16]{0:T(128)S(1)}, f32[16]{0:T(128)}, u32[]{:S(2)}) copy-start(f32[16]{0:T(128)} %get-tuple-element.429) | copy-start | bytes 196
Sparse Core Ops, SparseCore 0:
  11.6 67.1 all-gather.3
where the time goes:
time: 842 us; the launch traced here: 831 us
  blocking collectives  302 us (36%)
  waiting for transfers between devices  252 us (30%)
  local copies, waits for them, and re-layouts  145 us (17%)
  other arithmetic  54.5 us (6%)
  starting transfers between devices  34.3 us (4%)
  matrix products  27.2 us (3%)
  between operations  15.5 us (2%)
    ppermute x4, waiting for transfers between devices, from_behind(): return lax.ppermute(block, axis, route)  187 us
    unnamed x1, blocking collectives  85 us
    all_gather x4, blocking collectives, local(): received = lax.all_gather(moved, 'tensor', axis=1, tiled=True)  84.8 us
    psum x1, blocking collectives, local(): lax.psum(lax.psum(jnp.stack([scale_part, gain_part]), 'tensor'), 'dp')  71.2 us
    all_gather x1, waiting for transfers between devices, local(): lax.all_gather(master[0].astype(jnp.bfloat16), 'dp', axis=0, tiled=True)  50.3 us
    another operation x23, local copies, waits for them, and re-layouts  32.2 us
    psum x1, blocking collectives, local(): lax.psum(jnp.stack([scale_part, gain_part]), 'tensor')  27 us
    dynamic_update_slice x15, local copies, waits for them, and re-layouts, store_slot(): return lax.dynamic_update_index_in_dim(buffer, value, slot_index, 0)  22.6 us
  transfers between devices with their start and end apart: 11, of which 8 were waited for; matrix products, arithmetic and copies ran while one was open for 16% of the time, Pallas kernels for 0%

commit v1 on v0

--- a/solution.py
+++ b/solution.py
@@ -48,7 +48,24 @@
     score_root = math.sqrt(HD)
     scale_vec = layer_scale[0]
     gain_vec = norm_gain[0]
-    weights = lax.all_gather(master[0].astype(jnp.bfloat16), "dp", axis=0, tiled=True)
+    value_2 = master[0].astype(jnp.bfloat16)
+    size, index, width = (lax.axis_size("dp"), lax.axis_index("dp"), value_2.shape[0])
+    ahead = [(i_2, (i_2 + 1) % size) for i_2 in range(size)]
+    downward = [(i_2, (i_2 - 1) % size) for i_2 in range(size)]
+    weights = jnp.zeros((*value_2.shape[:0], size * width, *value_2.shape[0 + 1 :]), value_2.dtype)
+    weights = lax.dynamic_update_slice_in_dim(weights, value_2, index * width, axis=0)
+    from_left = from_right = value_2
+    half = size // 2
+    for step in range(1, half + 1):
+        from_left = lax.ppermute(from_left, "dp", ahead)
+        weights = lax.dynamic_update_slice_in_dim(
+            weights, from_left, (index - step) % size * width, axis=0
+        )
+        if step < size - half:
+            from_right = lax.ppermute(from_right, "dp", downward)
+            weights = lax.dynamic_update_slice_in_dim(
+                weights, from_right, (index + step) % size * width, axis=0
+            )
     w_qkv = weights[:, : 3 * head_cols]
     w_out = weights[:, 3 * head_cols :]
     full_x = lax.all_gather(x_in[0], "tensor", axis=2, tiled=True).astype(jnp.float32)

time: 842 us -> 889 us (1.056)
  starting transfers between devices: 34.3 us -> 111 us
  waiting for transfers between devices: 252 us -> 204 us
  local copies, waits for them, and re-layouts: 145 us -> 171 us
  between operations: 15.5 us -> 2.34 us
    ppermute x0 -> x15, starting transfers between devices: none -> 66.1 us  [the longest x7 49.3 us: local(): from_right = lax.ppermute(from_right, 'dp', downward)]
    all_gather x1 -> x0, waiting for transfers between devices: 50.3 us -> none  [local(): lax.all_gather(master[0].astype(jnp.bfloat16), 'dp', axis=0, tiled=True)]
    dynamic_update_slice x0 -> x16, local copies, waits for them, and re-layouts: none -> 29 us  [the longest x8 14.5 us: local(): lax.dynamic_update_slice_in_dim(weights, from_left, (index - step) % size...]
    ppermute x0 -> x15, waiting for transfers between devices: none -> 11.1 us  [the longest x8 11.1 us: local(): from_left = lax.ppermute(from_left, 'dp', ahead)]
    ppermute x4, starting transfers between devices: 8.4 us -> 18 us  [from_behind(): return lax.ppermute(block, axis, route)]
  transfers between devices with their start and end apart: 11 -> 25, of which waited for: 8 -> 12; matrix products, arithmetic and copies ran while one was open for 16% -> 19% of each run, Pallas kernels for 0% -> 0%
where the time goes in v1:
time: 889 us; the launch traced here: 876 us
  blocking collectives  305 us (34%)
  waiting for transfers between devices  204 us (23%)
  local copies, waits for them, and re-layouts  171 us (19%)
  starting transfers between devices  111 us (12%)
  other arithmetic  55.8 us (6%)
  matrix products  27.2 us (3%)
    ppermute x4, waiting for transfers between devices, from_behind(): return lax.ppermute(block, axis, route)  180 us
    unnamed x1, blocking collectives  87.5 us
    all_gather x4, blocking collectives, local(): received = lax.all_gather(moved, 'tensor', axis=1, tiled=True)  84.8 us
    psum x1, blocking collectives, local(): lax.psum(lax.psum(jnp.stack([scale_part, gain_part]), 'tensor'), 'dp')  71 us
    ppermute x7, starting transfers between devices, local(): from_right = lax.ppermute(from_right, 'dp', downward)  49.3 us
    another operation x23, local copies, waits for them, and re-layouts  33.3 us
    psum x1, blocking collectives, local(): lax.psum(jnp.stack([scale_part, gain_part]), 'tensor')  27.2 us
    dynamic_update_slice x15, local copies, waits for them, and re-layouts, store_slot(): return lax.dynamic_update_index_in_dim(buffer, value, slot_index, 0)  22.5 us
  transfers between devices with their start and end apart: 25, of which 12 were waited for; matrix products, arithmetic and copies ran while one was open for 19% of the time, Pallas kernels for 0%

profile of v1, /device:TPU:128, one launch (start us, length us, event | category | flops | bytes accessed | tf_op | source)
XLA Modules:
  0.0 876.4 jit_solution(5914497277587601556)
XLA Ops:
  1.8 3.4 collective-permute-start
  5.2 5.8 collective-permute-start.1
  11.0 3.2 collective-permute-done
  16.1 7.2 collective-permute-start.3
  23.3 2.3 collective-permute-done.2
  27.6 7.2 collective-permute-start.5
  38.6 7.2 collective-permute-start.7
  49.7 7.3 collective-permute-start.9
  60.8 17.7 %all-gather = bf16[1,2,1,128,1600]{4,3,2,1,0:T(8,128)(2,1)S(1)} all-gather(bf16[1,2,1,16,1600]{4,3,2,1,0:T(8,128)(2,1)} %param.17), channel_id=2, replica_groups=mesh['pipe'=4,'dp'=16,'tensor'=8] {'tensor'}, dimensions={3}, use_global_device_ids=true | all-gather | bytes 921600 | tf_op jit(solution)/shard_map/all_gather | solution.py:71
  78.6 7.3 collective-permute-start.11
  94.3 7.2 collective-permute-start.13
  130.7 2.6 fusion.113
  142.9 2.3 conditional.5
  147.2 5.0 all-to-all-start
  153.9 2.5 convert_multiply_fusion.6
  156.4 9.2 %all-to-all-done = bf16[1,8,16,1600]{3,2,0,1:T(8,128)(2,1)} async-done(((bf16[1,8,16,1600]{3,2,0,1:T(8,128)(2,1)}), bf16[1,8,16,1600]{3,2,0,1:T(8,128)(2,1)}, u32[]{:S(2)}, u32[]{:S(2)}) %all-to-all-start) | async-done | bytes 409632 | tf_op jit(solution)/shard_map/all_to_all | solution.py:155
  169.4 2.2 fusion.162
  177.7 6.9 collective-permute-start.15
  184.7 35.3 %collective-permute-done.15 = bf16[1,16,1600]{1,2,0:T(8,128)(2,1)} collective-permute-done((bf16[1,16,1600]{1,2,0:T(8,128)(2,1)}, bf16[1,16,1600]{1,2,0:T(8,128)(2,1)}, u32[]{:S(2)}, u32[]{:S(2)}) %collective-permute-start.15) | collective-permute-done | bytes 51232 | tf_op jit(solution)/shard_map/ppermute | solution.py:20
  221.8 15.8 %all_gather.16 = bf16[1,128,1600]{2,1,0:T(8,128)(2,1)} all-gather(bf16[1,16,1600]{2,1,0:T(8,128)(2,1)} %copy.219), channel_id=1, replica_groups=mesh['pipe'=4,'dp'=16,'tensor'=8] {'tensor'}, dimensions={1}, use_global_device_ids=true | all-gather | bytes 460800 | tf_op jit(solution)/shard_map/all_gather | solution.py:172
  239.5 2.2 bitcast_dynamic-update-slice_fusion.2
  241.7 2.3 conditional.6
  245.9 16.6 %all_to_all.25 = bf16[1,8,16,1600]{3,2,0,1:T(8,128)(2,1)S(1)} all-to-all(bf16[1,8,16,1600]{3,2,0,1:T(8,128)(2,1)} %bitcast.587), channel_id=1, replica_groups=mesh['pipe'=4,'dp'=16,'tensor'=8] {'tensor'}, dimensions={1} | all-to-all | bytes 819200 | tf_op jit(solution)/shard_map/all_to_all | solution.py:155
  263.2 2.2 fusion.161
  273.6 7.0 collective-permute-start.16
  280.6 90.9 %collective-permute-done.16 = bf16[1,16,1600]{1,2,0:T(8,128)(2,1)} collective-permute-done((bf16[1,16,1600]{1,2,0:T(8,128)(2,1)}, bf16[1,16,1600]{1,2,0:T(8,128)(2,1)}, u32[]{:S(2)}, u32[]{:S(2)}) %collective-permute-start.16) | collective-permute-done | bytes 51232 | tf_op jit(solution)/shard_map/ppermute | solution.py:20
  373.3 15.8 %all_gather.17 = bf16[1,128,1600]{2,1,0:T(8,128)(2,1)} all-gather(bf16[1,16,1600]{2,1,0:T(8,128)(2,1)} %copy.234), channel_id=1, replica_groups=mesh['pipe'=4,'dp'=16,'tensor'=8] {'tensor'}, dimensions={1}, use_global_device_ids=true | all-gather | bytes 460800 | tf_op jit(solution)/shard_map/all_gather | solution.py:172
  391.1 2.2 bitcast_dynamic-update-slice_fusion.1
  393.2 32.0 %conditional.7 = (bf16[1,128,1600]{1,2,0:T(8,128)(2,1)}, bf16[1,1,128,768]{3,2,0,1:T(8,128)(2,1)}, bf16[1,1,128,1600]{2,3,0,1:T(8,128)(2,1)}) conditional(s32[]{:T(128)} %convert_element_type.339, () %tuple.72, (s32[]{:T(128)}, bf16[2,1,128,2,128]{4,2,3,0,1:T(8,128)(2,1)}, f32[2,1,2,128,128]{3,4,2,0,1:T(8,128)S(1)}, f32[1,1600]{1,0:T(1,128)S(1)}, ...), branch_computations={%region_11.12_spmd, %region_12.13_spmd} | conditional | flops 454803200 | bytes 11565162 | solution.py:151
  427.2 4.3 all-to-all-start.2
  440.7 4.0 all-to-all-done.2
  446.4 2.2 fusion.160
  460.1 38.8 %collective-permute-done.17 = bf16[1,16,1600]{1,2,0:T(8,128)(2,1)} collective-permute-done((bf16[1,16,1600]{1,2,0:T(8,128)(2,1)S(1)}, bf16[1,16,1600]{1,2,0:T(8,128)(2,1)}, u32[]{:S(2)}, u32[]{:S(2)}) %collective-permute-start.17) | collective-permute-done | bytes 51232 | tf_op jit(solution)/shard_map/ppermute | solution.py:20
  500.7 15.8 %all_gather.18 = bf16[1,128,1600]{2,1,0:T(8,128)(2,1)} all-gather(bf16[1,16,1600]{2,1,0:T(8,128)(2,1)} %copy.249), channel_id=1, replica_groups=mesh['pipe'=4,'dp'=16,'tensor'=8] {'tensor'}, dimensions={1}, use_global_device_ids=true | all-gather | bytes 460800 | tf_op jit(solution)/shard_map/all_gather | solution.py:172
  520.6 32.0 %conditional.8 = (bf16[1,128,1600]{1,2,0:T(8,128)(2,1)}, bf16[1,1,128,768]{3,2,0,1:T(8,128)(2,1)}, bf16[1,1,128,1600]{2,3,0,1:T(8,128)(2,1)}) conditional(s32[]{:T(128)} %convert_element_type.344, () %tuple.74, (s32[]{:T(128)}, bf16[2,1,128,2,128]{4,2,3,0,1:T(8,128)(2,1)}, f32[2,1,2,128,128]{3,4,2,0,1:T(8,128)S(1)}, f32[1,1600]{1,0:T(1,128)S(1)}, ...), branch_computations={%region_15.16_spmd, %region_16.17_spmd} | conditional | flops 454803200 | bytes 11565162 | solution.py:151
  554.6 4.1 all-to-all-start.3
  587.5 2.2 collective-permute-start.18
  592.9 14.5 %collective-permute-done.18 = bf16[1,16,1600]{1,2,0:T(8,128)(2,1)} collective-permute-done((bf16[1,16,1600]{1,2,0:T(8,128)(2,1)}, bf16[1,16,1600]{1,2,0:T(8,128)(2,1)}, u32[]{:S(2)}, u32[]{:S(2)}) %collective-permute-start.18) | collective-permute-done | bytes 51232 | tf_op jit(solution)/shard_map/ppermute | solution.py:20
  609.2 37.4 %all_gather.19 = bf16[1,128,1600]{2,1,0:T(8,128)(2,1)} all-gather(bf16[1,16,1600]{2,1,0:T(8,128)(2,1)} %copy.264), channel_id=1, replica_groups=mesh['pipe'=4,'dp'=16,'tensor'=8] {'tensor'}, dimensions={1}, use_global_device_ids=true | all-gather | bytes 460800 | tf_op jit(solution)/shard_map/all_gather | solution.py:172
  648.6 2.2 bitcast_dynamic-update-slice_fusion.3
  650.8 2.3 conditional.9
  655.1 5.3 all-to-all-start.4
  667.4 2.2 pad_maximum_fusion.5
  669.6 87.5 %fusion = bf16[112,1024]{1,0:T(8,128)(2,1)S(1)} fusion(bf16[1600,1024]{1,0:T(8,128)(2,1)} %pad_maximum_fusion.5), kind=kCustom, calls=%all-reduce-scatter | all-reduce-scatter fusion | flops 1835009 | bytes 3508224
  757.2 3.6 collective-permute-start.19
  760.7 4.1 collective-permute-start.20
  774.6 27.2 %psum.14 = f32[2,1600]{1,0:T(2,128)S(1)} all-reduce(f32[2,1600]{1,0:T(2,128)S(1)} %pad_maximum_fusion.6), channel_id=1, replica_groups=mesh['pipe'=4,'dp'=16,'tensor'=8] {'tensor'}, use_global_device_ids=true, to_apply=%region_30.31 | all-reduce | flops 3200 | bytes 25600 | tf_op jit(solution)/shard_map/psum | solution.py:191
  801.8 71.0 %psum.15 = f32[1,2,1600]{2,1,0:T(2,128)} all-reduce(f32[1,2,1600]{2,1,0:T(2,128)S(1)} %bitcast.592), channel_id=1, replica_groups=mesh['pipe'=4,'dp'=16,'tensor'=8] {'dp'}, use_global_device_ids=true, to_apply=%region_31.32 | all-reduce | flops 3200 | bytes 25600 | tf_op jit(solution)/shard_map/psum | solution.py:191
  (263 shorter events, 255.2 us)
Async XLA Ops:
  0.6 88.4 %copy-start.10 = (bf16[2,1,128,1600]{2,3,1,0:T(8,128)(2,1)S(1)}, bf16[2,1,128,1600]{2,3,1,0:T(8,128)(2,1)}, u32[]{:S(2)}) copy-start(bf16[2,1,128,1600]{2,3,1,0:T(8,128)(2,1)} %param.18) | copy-start | bytes 2457604
  1.8 12.4 %collective-permute-start = (bf16[100,1024]{1,0:T(8,128)(2,1)S(1)}, bf16[100,1024]{1,0:T(8,128)(2,1)S(1)}, u32[]{:S(2)}, u32[]{:S(2)}) collective-permute-start(bf16[100,1024]{1,0:T(8,128)(2,1)S(1)} %bitcast.589), channel_id=1, source_target_pairs={{0,8},{8,16},{16,24},{24,32},{32,40},{40,48},{48,56},{56,64},{64,7... | collective-permute-start | bytes 614408 | tf_op jit(solution)/shard_map/ppermute | solution.py:60
  5.2 10.9 %collective-permute-start.1 = (bf16[100,1024]{1,0:T(8,128)(2,1)S(1)}, bf16[100,1024]{1,0:T(8,128)(2,1)S(1)}, u32[]{:S(2)}, u32[]{:S(2)}) collective-permute-start(bf16[100,1024]{1,0:T(8,128)(2,1)S(1)} %bitcast.590), channel_id=1, source_target_pairs={{0,120},{8,0},{16,8},{24,16},{32,24},{40,32},{48,40},{56,48},{64,5... | collective-permute-start | bytes 614408 | tf_op jit(solution)/shard_map/ppermute | solution.py:65
  14.2 11.5 %collective-permute-start.2 = (bf16[100,1024]{1,0:T(8,128)(2,1)S(1)}, bf16[100,1024]{1,0:T(8,128)(2,1)S(1)}, u32[]{:S(2)}, u32[]{:S(2)}) collective-permute-start(bf16[100,1024]{1,0:T(8,128)(2,1)S(1)} %collective-permute-done), channel_id=1, source_target_pairs={{0,8},{8,16},{16,24},{24,32},{32,40},{40,48},{48,56},{56,64},{64,7... | collective-permute-start | bytes 614408 | tf_op jit(solution)/shard_map/ppermute | solution.py:60
  16.1 11.5 %collective-permute-start.3 = (bf16[100,1024]{1,0:T(8,128)(2,1)S(1)}, bf16[100,1024]{1,0:T(8,128)(2,1)S(1)}, u32[]{:S(2)}, u32[]{:S(2)}) collective-permute-start(bf16[100,1024]{1,0:T(8,128)(2,1)S(1)} %collective-permute-done.1), channel_id=1, source_target_pairs={{0,120},{8,0},{16,8},{24,16},{32,24},{40,32},{48,40},{56,48},{64,5... | collective-permute-start | bytes 614408 | tf_op jit(solution)/shard_map/ppermute | solution.py:65
  25.6 11.0 %collective-permute-start.4 = (bf16[100,1024]{1,0:T(8,128)(2,1)S(1)}, bf16[100,1024]{1,0:T(8,128)(2,1)S(1)}, u32[]{:S(2)}, u32[]{:S(2)}) collective-permute-start(bf16[100,1024]{1,0:T(8,128)(2,1)S(1)} %collective-permute-done.2), channel_id=1, source_target_pairs={{0,8},{8,16},{16,24},{24,32},{32,40},{40,48},{48,56},{56,64},{64,7... | collective-permute-start | bytes 614408 | tf_op jit(solution)/shard_map/ppermute | solution.py:60
  27.6 11.0 %collective-permute-start.5 = (bf16[100,1024]{1,0:T(8,128)(2,1)S(1)}, bf16[100,1024]{1,0:T(8,128)(2,1)S(1)}, u32[]{:S(2)}, u32[]{:S(2)}) collective-permute-start(bf16[100,1024]{1,0:T(8,128)(2,1)S(1)} %collective-permute-done.3), channel_id=1, source_target_pairs={{0,120},{8,0},{16,8},{24,16},{32,24},{40,32},{48,40},{56,48},{64,5... | collective-permute-start | bytes 614408 | tf_op jit(solution)/shard_map/ppermute | solution.py:65
  36.7 11.0 %collective-permute-start.6 = (bf16[100,1024]{1,0:T(8,128)(2,1)S(1)}, bf16[100,1024]{1,0:T(8,128)(2,1)S(1)}, u32[]{:S(2)}, u32[]{:S(2)}) collective-permute-start(bf16[100,1024]{1,0:T(8,128)(2,1)S(1)} %collective-permute-done.4), channel_id=1, source_target_pairs={{0,8},{8,16},{16,24},{24,32},{32,40},{40,48},{48,56},{56,64},{64,7... | collective-permute-start | bytes 614408 | tf_op jit(solution)/shard_map/ppermute | solution.py:60
  38.6 11.1 %collective-permute-start.7 = (bf16[100,1024]{1,0:T(8,128)(2,1)S(1)}, bf16[100,1024]{1,0:T(8,128)(2,1)}, u32[]{:S(2)}, u32[]{:S(2)}) collective-permute-start(bf16[100,1024]{1,0:T(8,128)(2,1)S(1)} %collective-permute-done.5), channel_id=1, source_target_pairs={{0,120},{8,0},{16,8},{24,16},{32,24},{40,32},{48,40},{56,48},{64,5... | collective-permute-start | bytes 614408 | tf_op jit(solution)/shard_map/ppermute | solution.py:65
  47.7 11.2 %collective-permute-start.8 = (bf16[100,1024]{1,0:T(8,128)(2,1)S(1)}, bf16[100,1024]{1,0:T(8,128)(2,1)}, u32[]{:S(2)}, u32[]{:S(2)}) collective-permute-start(bf16[100,1024]{1,0:T(8,128)(2,1)S(1)} %collective-permute-done.6), channel_id=1, source_target_pairs={{0,8},{8,16},{16,24},{24,32},{32,40},{40,48},{48,56},{56,64},{64,7... | collective-permute-start | bytes 614408 | tf_op jit(solution)/shard_map/ppermute | solution.py:60
  49.7 28.9 %collective-permute-start.9 = (bf16[100,1024]{1,0:T(8,128)(2,1)}, bf16[100,1024]{1,0:T(8,128)(2,1)}, u32[]{:S(2)}, u32[]{:S(2)}) collective-permute-start(bf16[100,1024]{1,0:T(8,128)(2,1)} %collective-permute-done.7), channel_id=1, source_target_pairs={{0,120},{8,0},{16,8},{24,16},{32,24},{40,32},{48,40},{56,48},{64,5... | collective-permute-start | bytes 614408 | tf_op jit(solution)/shard_map/ppermute | solution.py:65
  58.9 26.9 %collective-permute-start.10 = (bf16[100,1024]{1,0:T(8,128)(2,1)}, bf16[100,1024]{1,0:T(8,128)(2,1)}, u32[]{:S(2)}, u32[]{:S(2)}) collective-permute-start(bf16[100,1024]{1,0:T(8,128)(2,1)} %collective-permute-done.8), channel_id=1, source_target_pairs={{0,8},{8,16},{16,24},{24,32},{32,40},{40,48},{48,56},{56,64},{64,7... | collective-permute-start | bytes 614408 | tf_op jit(solution)/shard_map/ppermute | solution.py:60
  78.6 52.1 %copy-start = (bf16[1,2,1,128,1600]{4,3,2,1,0:T(8,128)(2,1)}, bf16[1,2,1,128,1600]{4,3,2,1,0:T(8,128)(2,1)S(1)}, u32[]{:S(2)}) copy-start(bf16[1,2,1,128,1600]{4,3,2,1,0:T(8,128)(2,1)S(1)} %all-gather) | copy-start | bytes 2457604
  78.6 11.5 %copy-start.39 = (f32[1,1600]{1,0:T(1,128)S(1)}, f32[1,1600]{1,0:T(1,128)}, u32[]{:S(2)}) copy-start(f32[1,1600]{1,0:T(1,128)} %param.20) | copy-start | bytes 19204
  78.6 15.7 %collective-permute-start.11 = (bf16[100,1024]{1,0:T(8,128)(2,1)}, bf16[100,1024]{1,0:T(8,128)(2,1)}, u32[]{:S(2)}, u32[]{:S(2)}) collective-permute-start(bf16[100,1024]{1,0:T(8,128)(2,1)} %collective-permute-done.9), channel_id=1, source_target_pairs={{0,120},{8,0},{16,8},{24,16},{32,24},{40,32},{48,40},{56,48},{64,5... | collective-permute-start | bytes 614408 | tf_op jit(solution)/shard_map/ppermute | solution.py:65
  85.8 15.7 %collective-permute-start.12 = (bf16[100,1024]{1,0:T(8,128)(2,1)}, bf16[100,1024]{1,0:T(8,128)(2,1)}, u32[]{:S(2)}, u32[]{:S(2)}) collective-permute-start(bf16[100,1024]{1,0:T(8,128)(2,1)} %collective-permute-done.10), channel_id=1, source_target_pairs={{0,8},{8,16},{16,24},{24,32},{32,40},{40,48},{48,56},{56,64},{64,7... | collective-permute-start | bytes 614408 | tf_op jit(solution)/shard_map/ppermute | solution.py:60
  94.3 32.8 %collective-permute-start.13 = (bf16[100,1024]{1,0:T(8,128)(2,1)}, bf16[100,1024]{1,0:T(8,128)(2,1)S(1)}, u32[]{:S(2)}, u32[]{:S(2)}) collective-permute-start(bf16[100,1024]{1,0:T(8,128)(2,1)} %collective-permute-done.11), channel_id=1, source_target_pairs={{0,120},{8,0},{16,8},{24,16},{32,24},{40,32},{48,40},{56,48},{64,5... | collective-permute-start | bytes 614408 | tf_op jit(solution)/shard_map/ppermute | solution.py:65
  101.5 27.4 %collective-permute-start.14 = (bf16[100,1024]{1,0:T(8,128)(2,1)}, bf16[100,1024]{1,0:T(8,128)(2,1)S(1)}, u32[]{:S(2)}, u32[]{:S(2)}) collective-permute-start(bf16[100,1024]{1,0:T(8,128)(2,1)} %collective-permute-done.12), channel_id=1, source_target_pairs={{0,8},{8,16},{16,24},{24,32},{32,40},{40,48},{48,56},{56,64},{64,7... | collective-permute-start | bytes 614408 | tf_op jit(solution)/shard_map/ppermute | solution.py:60
  103.5 27.2 %copy-start.37 = (f32[2,128]{1,0:T(2,128)}, f32[2,128]{1,0:T(2,128)S(1)}, u32[]{:S(2)}) copy-start(f32[2,128]{1,0:T(2,128)S(1)} %add_rsqrt_fusion) | copy-start | bytes 3076
  139.1 3.9 copy-start.31
  139.2 2.1 copy-start.12
  147.2 18.3 %all-to-all-start = ((bf16[1,8,16,1600]{3,2,0,1:T(8,128)(2,1)}), bf16[1,8,16,1600]{3,2,0,1:T(8,128)(2,1)}, u32[]{:S(2)}, u32[]{:S(2)}) async-start(bf16[1,8,16,1600]{3,2,0,1:T(8,128)(2,1)} %bitcast.584), calls=%async_computation | async-start | bytes 851968 | tf_op jit(solution)/shard_map/all_to_all | solution.py:155
  173.7 1.9 copy-start.6
  177.7 42.3 %collective-permute-start.15 = (bf16[1,16,1600]{1,2,0:T(8,128)(2,1)}, bf16[1,16,1600]{1,2,0:T(8,128)(2,1)}, u32[]{:S(2)}, u32[]{:S(2)}) collective-permute-start(bf16[1,16,1600]{1,2,0:T(8,128)(2,1)} %fusion.119), channel_id=1, source_target_pairs={{128,0},{256,128},{384,256},{129,1},{257,129},{385,257},{130,2},{2... | collective-permute-start | bytes 153608 | tf_op jit(solution)/shard_map/ppermute | solution.py:20
  269.6 1.9 copy-start.7
  273.6 97.9 %collective-permute-start.16 = (bf16[1,16,1600]{1,2,0:T(8,128)(2,1)}, bf16[1,16,1600]{1,2,0:T(8,128)(2,1)}, u32[]{:S(2)}, u32[]{:S(2)}) collective-permute-start(bf16[1,16,1600]{1,2,0:T(8,128)(2,1)} %fusion.139), channel_id=1, source_target_pairs={{128,0},{256,128},{384,256},{129,1},{257,129},{385,257},{130,2},{2... | collective-permute-start | bytes 153608 | tf_op jit(solution)/shard_map/ppermute | solution.py:20
  427.2 17.5 %all-to-all-start.2 = ((bf16[1,8,16,1600]{3,2,0,1:T(8,128)(2,1)}), bf16[1,8,16,1600]{3,2,0,1:T(8,128)(2,1)}, u32[]{:S(2)}, u32[]{:S(2)}) async-start(bf16[1,8,16,1600]{3,2,0,1:T(8,128)(2,1)} %bitcast.585), calls=%async_computation.2 | async-start | bytes 851968 | tf_op jit(solution)/shard_map/all_to_all | solution.py:155
  452.8 1.8 copy-start.4
  452.8 1.9 copy-start.8
  454.6 4.8 copy-start.30
  456.9 42.0 %collective-permute-start.17 = (bf16[1,16,1600]{1,2,0:T(8,128)(2,1)S(1)}, bf16[1,16,1600]{1,2,0:T(8,128)(2,1)}, u32[]{:S(2)}, u32[]{:S(2)}) collective-permute-start(bf16[1,16,1600]{1,2,0:T(8,128)(2,1)S(1)} %fusion.134), channel_id=1, source_target_pairs={{128,0},{256,128},{384,256},{129,1},{257,129},{385,257},{130,2},{2... | collective-permute-start | bytes 153608 | tf_op jit(solution)/shard_map/ppermute | solution.py:20
  554.6 20.8 %all-to-all-start.3 = ((bf16[1,8,16,1600]{3,2,0,1:T(8,128)(2,1)}), bf16[1,8,16,1600]{3,2,0,1:T(8,128)(2,1)}, u32[]{:S(2)}, u32[]{:S(2)}) async-start(bf16[1,8,16,1600]{3,2,0,1:T(8,128)(2,1)} %bitcast.586), calls=%async_computation.3 | async-start | bytes 851968 | tf_op jit(solution)/shard_map/all_to_all | solution.py:155
  583.4 1.9 copy-start.9
  587.5 19.9 %collective-permute-start.18 = (bf16[1,16,1600]{1,2,0:T(8,128)(2,1)}, bf16[1,16,1600]{1,2,0:T(8,128)(2,1)}, u32[]{:S(2)}, u32[]{:S(2)}) collective-permute-start(bf16[1,16,1600]{1,2,0:T(8,128)(2,1)} %fusion.129), channel_id=1, source_target_pairs={{128,0},{256,128},{384,256},{129,1},{257,129},{385,257},{130,2},{2... | collective-permute-start | bytes 153608 | tf_op jit(solution)/shard_map/ppermute | solution.py:20
  653.1 9.0 %copy-start.1 = (bf16[1,2,1,128,1600]{4,3,2,1,0:T(8,128)(2,1)S(1)}, bf16[1,2,1,128,1600]{4,3,2,1,0:T(8,128)(2,1)}, u32[]{:S(2)}) copy-start(bf16[1,2,1,128,1600]{4,3,2,1,0:T(8,128)(2,1)} %copy-done) | copy-start | bytes 2457604
  653.1 9.0 %copy-start.38 = (f32[2,128]{1,0:T(2,128)S(1)}, f32[2,128]{1,0:T(2,128)}, u32[]{:S(2)}) copy-start(f32[2,128]{1,0:T(2,128)} %copy-done.37) | copy-start | bytes 3076
  655.1 118.0 %all-to-all-start.4 = ((bf16[1,8,16,1600]{3,2,0,1:T(8,128)(2,1)}), bf16[1,8,16,1600]{3,2,0,1:T(8,128)(2,1)S(1)}, u32[]{:S(2)}, u32[]{:S(2)}) async-start(bf16[1,8,16,1600]{3,2,0,1:T(8,128)(2,1)} %bitcast.151), calls=%async_computation.4 | async-start | bytes 851968 | tf_op jit(solution)/shard_map/all_to_all | solution.py:155
  662.1 3.7 copy-start.11
  757.2 10.3 %collective-permute-start.19 = (bf16[112,1024]{1,0:T(8,128)(2,1)S(1)}, bf16[112,1024]{1,0:T(8,128)(2,1)S(1)}, u32[]{:S(2)}, u32[]{:S(2)}) collective-permute-start(bf16[112,1024]{1,0:T(8,128)(2,1)S(1)} %fusion), channel_id=1, source_target_pairs={{0,8},{8,16},{16,24},{24,32},{32,40},{40,48},{48,56},{56,64},{64,7... | collective-permute-start | bytes 688136
  760.7 6.8 collective-permute-start.20
  764.8 3.3 copy-start.19
  764.9 3.3 copy-start.26
  770.8 3.7 copy-start.33
  770.8 3.7 copy-start.34
  770.8 3.7 copy-start.35
  770.8 3.7 copy-start.36
  774.2 99.2 %copy-start.13 = (bf16[1,128,1600]{1,2,0:T(8,128)(2,1)S(1)}, bf16[1,128,1600]{1,2,0:T(8,128)(2,1)}, u32[]{:S(2)}) copy-start(bf16[1,128,1600]{1,2,0:T(8,128)(2,1)} %get-tuple-element.402) | copy-start | bytes 1228804
  774.2 99.2 %copy-start.40 = (f32[16]{0:T(128)S(1)}, f32[16]{0:T(128)}, u32[]{:S(2)}) copy-start(f32[16]{0:T(128)} %get-tuple-element.429) | copy-start | bytes 196
  (11 other events, 11.1 us)
